TPU v7x, 32 devices: a whole 2x2x4 slice. The times are simulated.
32 devices in a mesh: gx: 2 (over x), gy: 4 (over z), cyc: 4 (over y, core).
Axes of the slice: x: 2, y: 2, z: 4, core: 2. Of those that a mesh axis runs over, the one named last changes fastest.
Arguments:
- displacement: bfloat16 [2, 48, 512, 1024], P(None, 'gx', 'gy', 'cyc'), may hold values from -6 to 6
Outputs:
- basis: float32 [2, 48, 512, 128], P(None, 'gx', 'gy', 'cyc')
All inputs are finite; a program needn't handle non-finite values.
Results may differ from a plain program's by a relative error of at most 0.0003.
Values may be sent and summed in bfloat16 or wider, within the bound.
A program may use at most 128 MiB of HBM per device.

v0:
```python
import jax
import jax.numpy as jnp
from jax import lax
from jax.sharding import PartitionSpec as P

RANK = 128
POWER = 3


def with_halo(block, sides, width):
    for axis, dim in sides:
        count = lax.axis_size(axis)
        forward = [(i, i + 1) for i in range(count - 1)]
        backward = [(target, source) for source, target in forward]
        low = lax.ppermute(
            lax.slice_in_dim(block, block.shape[dim] - width, None, axis=dim), axis, forward
        )
        high = lax.ppermute(lax.slice_in_dim(block, 0, width, axis=dim), axis, backward)
        block = jnp.concatenate([low, block, high], axis=dim)
    return block


def swapped(value, axis, stride):
    mask = 2**stride
    pairs = [(source, source ^ mask) for source in range(lax.axis_size(axis))]
    return lax.ppermute(value, axis, pairs)


def strain_rows(padded):
    field = padded.astype(jnp.float32)
    along_x = (field[:, 2:, 1:-1] - field[:, :-2, 1:-1]) * 0.5
    along_y = (field[:, 1:-1, 2:] - field[:, 1:-1, :-2]) * 0.5
    strain_xx = along_x[0]
    strain_yy = along_y[1]
    strain_xy = 0.5 * (along_x[1] + along_y[0])
    first = strain_xx + strain_yy
    second = strain_xx * strain_yy - strain_xy * strain_xy
    return jnp.stack([first, second]).reshape(-1, padded.shape[-1])


def gram_of(joined):
    return lax.dot_general(
        joined,
        joined,
        (((0,), (0,)), ((), ())),
        precision=lax.Precision.HIGHEST,
        preferred_element_type=jnp.float32,
    )


def matmul_high(left, right):
    return jnp.dot(left, right, precision=lax.Precision.HIGHEST, preferred_element_type=jnp.float32)


def vectors_of(gram):
    width = gram.shape[0]
    normed = gram / (jnp.trace(gram) / width + 1e-06)
    vectors = (jnp.arange(width)[:, None] % RANK == jnp.arange(RANK)[None, :]).astype(jnp.float32)
    for step in range(POWER):
        moved = matmul_high(normed, vectors)
        lower = jnp.linalg.cholesky(gram_of(moved))
        vectors = lax.linalg.triangular_solve(
            lower, moved, left_side=False, lower=True, transpose_a=True
        )
    return vectors


def finish(joined, gram):
    return matmul_high(joined, vectors_of(gram))


def truncate(joined):
    return finish(joined, lax.psum(gram_of(joined), ("gx", "gy")))


def own_columns(whole):
    groups = lax.axis_size("cyc")
    share = whole.shape[1] // groups
    return lax.dynamic_slice_in_dim(whole, lax.axis_index("cyc") * share, share, 1)


def on_device(displacement):
    padded = with_halo(displacement, (("gx", 1), ("gy", 2)), 1)
    local_rows = displacement.shape[1]
    local_cols = displacement.shape[2]
    piece = truncate(strain_rows(padded))
    group = lax.axis_index("cyc")
    for level in range(lax.axis_size("cyc").bit_length() - 1):
        partner = swapped(piece, "cyc", level)
        is_low = group >> level & 1 == 0
        first_half = jnp.where(is_low, piece, partner)
        second_half = jnp.where(is_low, partner, piece)
        piece = truncate(jnp.concatenate([first_half, second_half], axis=1))
    result = own_columns(piece)
    return result.reshape(2, local_rows, local_cols, result.shape[1])


def solution(mesh):
    return jax.shard_map(
        on_device,
        mesh=mesh,
        in_specs=(P(None, "gx", "gy", "cyc"),),
        out_specs=P(None, "gx", "gy", "cyc"),
        check_vma=False,
    )
```

profile of v0, /device:TPU:0, one launch (start us, length us, event | category | flops | bytes accessed | tf_op | source)
XLA Modules:
  0.0 619.7 jit_solution(6045375784740852423)
XLA Ops:
  7.5 4.8 collective-permute-start
  13.7 1.4 collective-permute-done
  15.1 2.2 constant_dynamic-update-slice_fusion.1
  17.4 1.9 collective-permute-done.1
  19.4 3.5 collective-permute-start.2
  24.6 4.3 collective-permute-done.3
  30.0 4.7 fusion.1
  34.7 4.0 slice_add_fusion.1
  38.7 1.7 copy-done
  40.4 10.9 %convolution_bitcast_fusion = f32[256,256]{1,0:T(8,128)} fusion(f32[1,24,128,256]{3,2,1,0:T(8,128)S(1)} %get-tuple-element.8, f32[1,24,128,256]{3,2,1,0:T(8,128)S(1)} %get-tuple-element.6), kind=kOutput, calls=%fused_computation.21 | convolution fusion | flops 4833411072 | bytes 6553600 | tf_op jit(solution)/shard_map/dot_general | solution.py:42
  51.6 5.1 pad_maximum_fusion
  56.8 64.7 %all-reduce.4.cloned.1.call-done = f32[256,256]{1,0:T(8,128)} async-done(((f32[256,256]{1,0:T(8,128)}), f32[256,256]{1,0:T(8,128)}) %all-reduce.4.cloned.1.call-update) | async-done | bytes 262160 | tf_op jit(solution)/shard_map/psum | solution.py:73
  121.4 1.7 select_reduce_fusion.2
  125.6 11.7 %cholesky.149 = f32[128,128]{1,0:T(8,128)S(1)} custom-call(f32[128,128]{1,0:T(8,128)S(1)} %fusion.38), custom_call_target="Cholesky" | custom-call | tf_op jit(solution)/shard_map/jit(cholesky)/cholesky | solution.py:61
  138.6 9.8 %custom-call.13 = f32[1,128,128]{1,2,0:T(8,128)S(1)} custom-call(f32[1,128,128]{2,1,0:T(8,128)S(1)} %fusion.12), custom_call_target="InvertDiagBlocksLowerTriangular" | custom-call | tf_op jit(solution)/shard_map/triangular_solve/custom-call.0 | solution.py:62
  150.6 11.7 %cholesky.160 = f32[128,128]{1,0:T(8,128)S(1)} custom-call(f32[128,128]{1,0:T(8,128)S(1)} %fusion.36), custom_call_target="Cholesky" | custom-call | tf_op jit(solution)/shard_map/jit(cholesky)/cholesky | solution.py:61
  164.0 9.8 %custom-call.14 = f32[1,128,128]{1,2,0:T(8,128)S(1)} custom-call(f32[1,128,128]{2,1,0:T(8,128)S(1)} %fusion.13), custom_call_target="InvertDiagBlocksLowerTriangular" | custom-call | tf_op jit(solution)/shard_map/triangular_solve/custom-call.0 | solution.py:62
  175.1 11.7 %cholesky.171 = f32[128,128]{1,0:T(8,128)S(1)} custom-call(f32[128,128]{1,0:T(8,128)S(1)} %fusion.34), custom_call_target="Cholesky" | custom-call | tf_op jit(solution)/shard_map/jit(cholesky)/cholesky | solution.py:61
  188.1 9.8 %custom-call.15 = f32[1,128,128]{1,2,0:T(8,128)S(1)} custom-call(f32[1,128,128]{2,1,0:T(8,128)S(1)} %fusion.14), custom_call_target="InvertDiagBlocksLowerTriangular" | custom-call | tf_op jit(solution)/shard_map/triangular_solve/custom-call.0 | solution.py:62
  198.3 8.8 %fusion.61 = f32[6144,128]{0,1:T(8,128)S(1)} fusion(f32[6144,256]{1,0:T(8,128)} %bitcast.147, f32[256,128]{0,1:T(8,128)S(1)} %convolution_bitcast_fusion.7), kind=kOutput, calls=%fused_computation.132 | convolution fusion | flops 2415919104 | bytes 9568256 | tf_op jit(solution)/shard_map/dot_general | solution.py:52
  207.2 1.6 copy-done.3
  208.8 4.2 collective-permute-done.4
  213.0 3.3 broadcast_select_fusion.1
  216.2 1.7 copy-done.2
  217.9 5.9 fusion.5
  224.1 69.7 %all-reduce.6.cloned.1.call-done = f32[256,256]{1,0:T(8,128)} async-done(((f32[256,256]{1,0:T(8,128)}), f32[256,256]{1,0:T(8,128)}) %all-reduce.6.cloned.1.call-update) | async-done | bytes 262160 | tf_op jit(solution)/shard_map/psum | solution.py:73
  293.8 1.6 select_reduce_fusion.1
  297.9 11.7 %cholesky.182 = f32[128,128]{1,0:T(8,128)S(1)} custom-call(f32[128,128]{1,0:T(8,128)S(1)} %fusion.32), custom_call_target="Cholesky" | custom-call | tf_op jit(solution)/shard_map/jit(cholesky)/cholesky | solution.py:61
  310.9 9.8 %custom-call.16 = f32[1,128,128]{1,2,0:T(8,128)S(1)} custom-call(f32[1,128,128]{2,1,0:T(8,128)S(1)} %fusion.15), custom_call_target="InvertDiagBlocksLowerTriangular" | custom-call | tf_op jit(solution)/shard_map/triangular_solve/custom-call.0 | solution.py:62
  322.9 11.7 %cholesky.193 = f32[128,128]{1,0:T(8,128)S(1)} custom-call(f32[128,128]{1,0:T(8,128)S(1)} %fusion.30), custom_call_target="Cholesky" | custom-call | tf_op jit(solution)/shard_map/jit(cholesky)/cholesky | solution.py:61
  336.0 10.2 %custom-call.17 = f32[1,128,128]{1,2,0:T(8,128)S(1)} custom-call(f32[1,128,128]{2,1,0:T(8,128)S(1)} %fusion.16), custom_call_target="InvertDiagBlocksLowerTriangular" | custom-call | tf_op jit(solution)/shard_map/triangular_solve/custom-call.0 | solution.py:62
  348.3 11.7 %cholesky.204 = f32[128,128]{1,0:T(8,128)S(1)} custom-call(f32[128,128]{1,0:T(8,128)S(1)} %fusion.28), custom_call_target="Cholesky" | custom-call | tf_op jit(solution)/shard_map/jit(cholesky)/cholesky | solution.py:61
  361.4 9.8 %custom-call.18 = f32[1,128,128]{1,2,0:T(8,128)S(1)} custom-call(f32[1,128,128]{2,1,0:T(8,128)S(1)} %fusion.17), custom_call_target="InvertDiagBlocksLowerTriangular" | custom-call | tf_op jit(solution)/shard_map/triangular_solve/custom-call.0 | solution.py:62
  371.5 7.5 %fusion.4 = f32[6144,128]{0,1:T(8,128)} fusion(f32[256,128]{0,1:T(8,128)S(1)} %convolution_bitcast_fusion.4, f32[6144,128]{0,1:T(8,128)} %copy-done.2, f32[6144,128]{0,1:T(8,128)S(1)} %get-tuple-element.13), kind=kOutput, calls=%fused_computation.9 | convolution fusion | flops 2417491968 | bytes 9568256 | tf_op jit(solution)/shard_map/dot_general | solution.py:52
  379.0 1.5 collective-permute-start.5
  380.4 66.9 %collective-permute-done.5 = f32[6144,128]{0,1:T(8,128)} collective-permute-done((f32[6144,128]{0,1:T(8,128)}, f32[6144,128]{0,1:T(8,128)}, u32[]{:S(2)}, u32[]{:S(2)}) %collective-permute-start.5) | collective-permute-done | bytes 3145760 | tf_op jit(solution)/shard_map/ppermute | solution.py:26
  447.3 3.3 broadcast_select_fusion.3
  450.6 1.7 copy-done.1
  452.3 5.9 fusion.3
  458.2 69.8 %all-reduce.8.cloned.1.call-done = f32[256,256]{1,0:T(8,128)} async-done(((f32[256,256]{1,0:T(8,128)}), f32[256,256]{1,0:T(8,128)}) %all-reduce.8.cloned.1.call-update) | async-done | bytes 262160 | tf_op jit(solution)/shard_map/psum | solution.py:73
  528.0 1.6 select_reduce_fusion
  532.1 11.7 %cholesky.215 = f32[128,128]{1,0:T(8,128)S(1)} custom-call(f32[128,128]{1,0:T(8,128)S(1)} %fusion.26), custom_call_target="Cholesky" | custom-call | tf_op jit(solution)/shard_map/jit(cholesky)/cholesky | solution.py:61
  545.1 10.0 %custom-call.19 = f32[1,128,128]{1,2,0:T(8,128)S(1)} custom-call(f32[1,128,128]{2,1,0:T(8,128)S(1)} %fusion.18), custom_call_target="InvertDiagBlocksLowerTriangular" | custom-call | tf_op jit(solution)/shard_map/triangular_solve/custom-call.0 | solution.py:62
  557.3 11.7 %cholesky.226 = f32[128,128]{1,0:T(8,128)S(1)} custom-call(f32[128,128]{1,0:T(8,128)S(1)} %fusion.24), custom_call_target="Cholesky" | custom-call | tf_op jit(solution)/shard_map/jit(cholesky)/cholesky | solution.py:61
  570.3 9.8 %custom-call.20 = f32[1,128,128]{1,2,0:T(8,128)S(1)} custom-call(f32[1,128,128]{2,1,0:T(8,128)S(1)} %fusion.19), custom_call_target="InvertDiagBlocksLowerTriangular" | custom-call | tf_op jit(solution)/shard_map/triangular_solve/custom-call.0 | solution.py:62
  582.3 12.0 %cholesky.237 = f32[128,128]{1,0:T(8,128)S(1)} custom-call(f32[128,128]{1,0:T(8,128)S(1)} %fusion.22), custom_call_target="Cholesky" | custom-call | tf_op jit(solution)/shard_map/jit(cholesky)/cholesky | solution.py:61
  595.6 9.8 %custom-call.21 = f32[1,128,128]{1,2,0:T(8,128)S(1)} custom-call(f32[1,128,128]{2,1,0:T(8,128)S(1)} %fusion.20), custom_call_target="InvertDiagBlocksLowerTriangular" | custom-call | tf_op jit(solution)/shard_map/triangular_solve/custom-call.0 | solution.py:62
  605.8 5.8 fusion.2
  (97 shorter events, 37.4 us)
Async XLA Ops:
  6.5 114.9 %all-reduce.4.cloned.1.call-start = ((), (), s32[]{:S(2)}) async-start(), calls=%async_computation | async-start | bytes 524288 | tf_op jit(solution)/shard_map/psum | solution.py:73
  7.5 7.6 %collective-permute-start = (bf16[2,1,128,256]{3,2,1,0:T(8,128)(2,1)S(1)}, bf16[2,1,128,256]{3,2,1,0:T(8,128)(2,1)S(1)}, u32[]{:S(2)}, u32[]{:S(2)}) collective-permute-start(bf16[2,1,128,256]{3,2,1,0:T(8,128)(2,1)S(1)} %get-tuple-element.18), channel_id=1, source_target_pairs={{0,16},{1,17},{2,18},{3,19},{4,20},{5,21},{6,22},{7,23},{8,24},{9,... | collective-permute-start | bytes 393224 | tf_op jit(solution)/shard_map/ppermute | solution.py:15
  12.4 6.9 %collective-permute-start.1 = (bf16[2,1,128,256]{3,2,1,0:T(8,128)(2,1)S(1)}, bf16[2,1,128,256]{3,2,1,0:T(8,128)(2,1)S(1)}, u32[]{:S(2)}, u32[]{:S(2)}) collective-permute-start(bf16[2,1,128,256]{3,2,1,0:T(8,128)(2,1)S(1)} %get-tuple-element.17), channel_id=1, source_target_pairs={{16,0},{17,1},{18,2},{19,3},{20,4},{21,5},{22,6},{23,7},{24,8},{25... | collective-permute-start | bytes 393224 | tf_op jit(solution)/shard_map/ppermute | solution.py:18
  19.4 5.3 collective-permute-start.2
  22.8 6.0 collective-permute-start.3
  38.7 1.7 copy-start
  51.4 242.5 %all-reduce.6.cloned.1.call-start = ((), (), s32[]{:S(2)}) async-start(), calls=%async_computation.1 | async-start | bytes 524288 | tf_op jit(solution)/shard_map/psum | solution.py:73
  121.4 52.7 %copy-start.4 = (f32[256,256]{1,0:T(8,128)S(1)}, f32[256,256]{1,0:T(8,128)}, u32[]{:S(2)}) copy-start(f32[256,256]{1,0:T(8,128)} %all-reduce.4.cloned.1.call-done) | copy-start | bytes 786436
  207.1 1.7 copy-start.3
  207.1 5.9 collective-permute-start.4
  216.2 1.7 copy-start.2
  223.8 304.2 %all-reduce.8.cloned.1.call-start = ((), (), s32[]{:S(2)}) async-start(), calls=%async_computation.2 | async-start | bytes 524288 | tf_op jit(solution)/shard_map/psum | solution.py:73
  379.0 68.4 %collective-permute-start.5 = (f32[6144,128]{0,1:T(8,128)}, f32[6144,128]{0,1:T(8,128)}, u32[]{:S(2)}, u32[]{:S(2)}) collective-permute-start(f32[6144,128]{0,1:T(8,128)} %fusion.4), channel_id=1, source_target_pairs={{0,2},{1,3},{2,0},{3,1},{4,6},{5,7},{6,4},{7,5},{8,10},{9,11},{10,... | collective-permute-start | bytes 9437192 | tf_op jit(solution)/shard_map/ppermute | solution.py:26
  450.6 1.7 copy-start.1
Sparse Core Ops, SparseCore 0:
  51.5 69.9 all-reduce.3
  224.0 69.8 all-reduce.5
  458.3 69.6 all-reduce.7
where the time goes:
time: 623 us; the launch traced here: 620 us
  waiting for transfers between devices  283 us (45%)
  other arithmetic  233 us (37%)
  matrix products  62 us (10%)
  between operations  16.4 us (3%)
  starting transfers between devices  13 us (2%)
  local copies, waits for them, and re-layouts  12 us (2%)
    psum x3, waiting for transfers between devices, truncate(): return finish(joined, lax.psum(gram_of(joined), ('gx', 'gy')))  204 us
    another operation x27, other arithmetic, vectors_of(): lower = jnp.linalg.cholesky(gram_of(moved))  112 us
    another operation x18, other arithmetic, vectors_of(): lax.linalg.triangular_solve(lower, moved, left_side=False, lower=True, tr...  94.7 us
    ppermute x2, waiting for transfers between devices, swapped(): return lax.ppermute(value, axis, pairs)  71.1 us
    dot_general x12, matrix products, matmul_high(): jnp.dot(left, right, precision=lax.Precision.HIGHEST, preferred_element_t...  33 us
    dot_general x12, matrix products, gram_of(): lax.dot_general(joined, joined, (((0,), (0,)), ((), ())), precision=lax.P...  26.2 us
  transfers between devices with their start and end apart: 9, of which 9 were waited for; matrix products, arithmetic and copies ran while one was open for 1% of the time, Pallas kernels for 0%

commit v1 on v0

v1 whole, which is shorter than its diff:
```python
import functools

import jax
import jax.numpy as jnp
from jax import lax
from jax.experimental import pallas as pl
from jax.experimental.pallas import tpu as pltpu
from jax.sharding import PartitionSpec as P

RANK = 128
POWER = 3
PANEL = 16
MESH = pl.DeviceIdType.MESH
HIGH = lax.Precision.HIGH
HIGHEST = lax.Precision.HIGHEST
VMEM_LIMIT = 48 * 1024 * 1024


def neighbours(block, axis, dim):
    count = lax.axis_size(axis)
    forward = [(i, i + 1) for i in range(count - 1)]
    backward = [(target, source) for source, target in forward]
    size = block.shape[dim]
    low = lax.ppermute(lax.slice_in_dim(block, size - 1, size, axis=dim), axis, forward)
    high = lax.ppermute(lax.slice_in_dim(block, 0, 1, axis=dim), axis, backward)
    return low, high


def exchanged(value, mask):
    pairs = [(source, source ^ mask) for source in range(lax.axis_size("cyc"))]
    return lax.ppermute(value, "cyc", pairs)


def contract(left, right, dims, precision=None):
    return lax.dot_general(
        left, right, (dims, ((), ())), precision=precision, preferred_element_type=jnp.float32
    )


def upper_blocks(gram_ref, full):
    gram_ref[0:RANK] = full[:RANK, :RANK]
    gram_ref[RANK : 2 * RANK] = full[:RANK, RANK:]
    gram_ref[2 * RANK : 3 * RANK] = full[RANK:, RANK:]
    if gram_ref.shape[0] > 3 * RANK:
        gram_ref[3 * RANK :] = jnp.zeros((gram_ref.shape[0] - 3 * RANK, RANK), jnp.float32)


def split(value):
    high = value.astype(jnp.bfloat16)
    return high, (value - high.astype(jnp.float32)).astype(jnp.bfloat16)


def add_gram(main, cross, value):
    high, low = split(value)
    main[...] += contract(high, high, ((0,), (0,)))
    cross[...] += contract(high, low, ((0,), (0,)))


def strain_kernel(u_ref, xlo_ref, xhi_ref, ylo_ref, yhi_ref, f_ref, gram_ref, main, cross):
    i = pl.program_id(0)
    rows = pl.num_programs(0)
    cols = u_ref.shape[2]

    @pl.when(i == 0)
    def _():
        main[...] = jnp.zeros_like(main)
        cross[...] = jnp.zeros_like(cross)

    node = lax.broadcasted_iota(jnp.int32, (cols, u_ref.shape[3]), 0)

    def dx(part):
        before = u_ref[part, jnp.maximum(i - 1, 0)].astype(jnp.float32)
        after = u_ref[part, jnp.minimum(i + 1, rows - 1)].astype(jnp.float32)
        before = jnp.where(i == 0, xlo_ref[part, 0].astype(jnp.float32), before)
        after = jnp.where(i == rows - 1, xhi_ref[part, 0].astype(jnp.float32), after)
        return (after - before) * 0.5

    def dy(part):
        here = u_ref[part, i].astype(jnp.float32)
        before = pltpu.roll(here, 1, 0)
        after = pltpu.roll(here, cols - 1, 0)
        before = jnp.where(node == 0, ylo_ref[part, i].astype(jnp.float32), before)
        after = jnp.where(node == cols - 1, yhi_ref[part, i].astype(jnp.float32), after)
        return (after - before) * 0.5

    exx = dx(0)
    eyy = dy(1)
    exy = (dx(1) + dy(0)) * 0.5
    first = exx + eyy
    second = exx * eyy - exy * exy
    f_ref[0, 0] = first
    f_ref[1, 0] = second
    add_gram(main, cross, first)
    add_gram(main, cross, second)

    @pl.when(i == rows - 1)
    def _():
        upper_blocks(gram_ref, main[...] + cross[...] + cross[...].T)


def strain(u, halo, padded):
    parts, rows, cols, width = u.shape
    whole = [pl.BlockSpec(a.shape, lambda i: (0, 0, 0, 0)) for a in (u, *halo)]
    return pl.pallas_call(
        strain_kernel,
        grid=(rows,),
        in_specs=whole,
        out_specs=[
            pl.BlockSpec((parts, 1, cols, width), lambda i: (0, i, 0, 0)),
            pl.BlockSpec((padded, RANK), lambda i: (0, 0)),
        ],
        out_shape=[
            jax.ShapeDtypeStruct((parts, rows, cols, width), jnp.float32),
            jax.ShapeDtypeStruct((padded, RANK), jnp.float32),
        ],
        scratch_shapes=[pltpu.VMEM((width, width), jnp.float32)] * 2,
        compiler_params=pltpu.CompilerParams(vmem_limit_bytes=VMEM_LIMIT),
    )(u, *halo)


def gram_kernel(left_ref, right_ref, gram_ref, main, cross):
    step = pl.program_id(0)

    @pl.when(step == 0)
    def _():
        main[...] = jnp.zeros_like(main)
        cross[...] = jnp.zeros_like(cross)

    add_gram(main, cross, jnp.concatenate([left_ref[...], right_ref[...]], axis=1))

    @pl.when(step == pl.num_programs(0) - 1)
    def _():
        upper_blocks(gram_ref, main[...] + cross[...] + cross[...].T)


def gram_of(left, right, padded):
    rows = left.shape[0]
    tile = 512 if rows % 512 == 0 else rows
    spec = pl.BlockSpec((tile, RANK), lambda i: (i, 0))
    return pl.pallas_call(
        gram_kernel,
        grid=(rows // tile,),
        in_specs=[spec, spec],
        out_specs=pl.BlockSpec((padded, RANK), lambda i: (0, 0)),
        out_shape=jax.ShapeDtypeStruct((padded, RANK), jnp.float32),
        scratch_shapes=[pltpu.VMEM((2 * RANK, 2 * RANK), jnp.float32)] * 2,
        compiler_params=pltpu.CompilerParams(vmem_limit_bytes=VMEM_LIMIT),
    )(left, right)


def sum_kernel(sizes, x_ref, o_ref, held, send_a, recv_a, send_b, recv_b):
    n_x, n_y, near = sizes
    n = n_x * n_y * near
    chunk = held.shape[1]
    cyc = lax.axis_index("cyc")
    base = cyc - lax.rem(cyc, near)
    me = (lax.axis_index("gx") * n_y + lax.axis_index("gy")) * near + lax.rem(cyc, near)

    def device(peer):
        plane = lax.div(peer, near)
        return (lax.div(plane, n_y), lax.rem(plane, n_y), base + lax.rem(peer, near))

    def chunk_at(ref, index):
        return ref.at[pl.ds(pl.multiple_of(index * chunk, 8), chunk)]

    def scatter(k):
        peer = lax.rem(me + k, n)
        return pltpu.make_async_remote_copy(
            src_ref=chunk_at(x_ref, peer), dst_ref=held.at[k],
            send_sem=send_a.at[k], recv_sem=recv_a.at[k],
            device_id=device(peer), device_id_type=MESH,
        )

    def gather(k):
        return pltpu.make_async_remote_copy(
            src_ref=chunk_at(o_ref, me), dst_ref=chunk_at(o_ref, me),
            send_sem=send_b.at[k], recv_sem=recv_b.at[k],
            device_id=device(lax.rem(me + k, n)), device_id_type=MESH,
        )

    def arrival(k):
        source = lax.rem(me - k + n, n)
        return pltpu.make_async_remote_copy(
            src_ref=chunk_at(o_ref, source), dst_ref=chunk_at(o_ref, source),
            send_sem=send_b.at[k], recv_sem=recv_b.at[k],
            device_id=device(source), device_id_type=MESH,
        )

    barrier = pltpu.get_barrier_semaphore()

    def loop(body):
        def step(k, carry):
            body(k)
            return carry

        lax.fori_loop(1, n, step, 0)

    loop(lambda k: pl.semaphore_signal(
        barrier, inc=1, device_id=device(lax.rem(me + k, n)), device_id_type=MESH))
    pl.semaphore_wait(barrier, n - 1)

    loop(lambda k: scatter(k).start())

    def added(k, total):
        scatter(k).wait_recv()
        return total + held[k]

    mine = pl.ds(pl.multiple_of(me * chunk, 8), chunk)
    o_ref[mine, :] = lax.fori_loop(1, n, added, x_ref[mine, :])
    loop(lambda k: gather(k).start())
    loop(lambda k: arrival(k).wait_recv())
    loop(lambda k: scatter(k).wait_send())
    loop(lambda k: gather(k).wait_send())


def group_size(near):
    return lax.axis_size("gx") * lax.axis_size("gy") * near


def padded_rows(near):
    n = group_size(near)
    chunk = -(-3 * RANK // (8 * n)) * 8
    return n * chunk


def summed(gram, near, ident):
    n = group_size(near)
    chunk = gram.shape[0] // n
    sizes = (lax.axis_size("gx"), lax.axis_size("gy"), near)
    return pl.pallas_call(
        functools.partial(sum_kernel, sizes),
        out_shape=jax.ShapeDtypeStruct(gram.shape, jnp.float32),
        in_specs=[pl.BlockSpec(memory_space=pltpu.VMEM)],
        out_specs=pl.BlockSpec(memory_space=pltpu.VMEM),
        scratch_shapes=[pltpu.VMEM((n, chunk, RANK), jnp.float32)]
        + [pltpu.SemaphoreType.DMA((n,))] * 4,
        compiler_params=pltpu.CompilerParams(
            collective_id=ident, has_side_effects=True, vmem_limit_bytes=VMEM_LIMIT
        ),
    )(gram)


def eliminate(work):
    parts = work.shape[1] // RANK
    for start in range(0, RANK, PANEL):
        rows = [
            [work[start + i : start + i + 1, p * RANK : (p + 1) * RANK] for p in range(parts)]
            for i in range(PANEL)
        ]
        block = [
            [
                jnp.broadcast_to(
                    work[start + i : start + i + 1, start + j : start + j + 1], (1, RANK)
                )
                for j in range(i + 1)
            ]
            for i in range(PANEL)
        ]
        for j in range(PANEL):
            scale = lax.rsqrt(block[j][j])
            rows[j] = [part * scale for part in rows[j]]
            column = {i: block[i][j] * scale for i in range(j + 1, PANEL)}
            for i in range(j + 1, PANEL):
                for k in range(j + 1, i + 1):
                    block[i][k] = block[i][k] - column[i] * column[k]
                rows[i] = [part - column[i] * top for part, top in zip(rows[i], rows[j])]
            for p in range(parts):
                work[start + j : start + j + 1, p * RANK : (p + 1) * RANK] = rows[j][p]
        after = start + PANEL
        if after < RANK:
            panel = work[start:after, :]
            work[after:, :] = work[after:, :] - contract(
                panel[:, after:RANK], panel, ((0,), (0,)), HIGHEST
            )


def vectors_kernel(gram_ref, v_ref, normed, work):
    width = 2 * RANK
    first = gram_ref[0:RANK]
    cross = gram_ref[RANK : 2 * RANK]
    last = gram_ref[2 * RANK : 3 * RANK]
    row = lax.broadcasted_iota(jnp.int32, (RANK, RANK), 0)
    col = lax.broadcasted_iota(jnp.int32, (RANK, RANK), 1)
    diagonal = jnp.where(row == col, first + last, 0.0)
    trace = jnp.sum(jnp.sum(diagonal, axis=0, keepdims=True), axis=1, keepdims=True)
    scale = 1.0 / (trace / width + 1e-06)
    normed[:RANK, :RANK] = first * scale
    normed[:RANK, RANK:] = cross * scale
    normed[RANK:, :RANK] = (cross * scale).T
    normed[RANK:, RANK:] = last * scale
    work[:, RANK:] = normed[:RANK, :] + normed[RANK:, :]

    def step(index, carry):
        @pl.when(index > 0)
        def _():
            work[:, RANK:] = contract(work[:, RANK:], normed[...], ((1,), (0,)), HIGHEST)

        moved = work[:, RANK:]
        work[:, :RANK] = contract(moved, moved, ((1,), (1,)), HIGHEST)
        eliminate(work)
        return carry

    lax.fori_loop(0, POWER, step, 0)
    v_ref[...] = work[:, RANK:]


def vectors_of(gram):
    return pl.pallas_call(
        vectors_kernel,
        out_shape=jax.ShapeDtypeStruct((RANK, 2 * RANK), jnp.float32),
        in_specs=[pl.BlockSpec(memory_space=pltpu.VMEM)],
        out_specs=pl.BlockSpec(memory_space=pltpu.VMEM),
        scratch_shapes=[
            pltpu.VMEM((2 * RANK, 2 * RANK), jnp.float32),
            pltpu.VMEM((RANK, 3 * RANK), jnp.float32),
        ],
        compiler_params=pltpu.CompilerParams(vmem_limit_bytes=VMEM_LIMIT),
    )(gram)


def on_device(displacement):
    groups = lax.axis_size("cyc")
    mine = lax.axis_index("cyc")
    low_bit = mine & 1
    side = mine >> 1
    parts, local_rows, local_cols, width = displacement.shape
    share = local_rows // groups
    halo = neighbours(displacement, "gx", 1) + neighbours(displacement, "gy", 2)
    field, gram = strain(displacement, halo, padded_rows(1))
    vectors = vectors_of(summed(gram, 1, 0))
    piece = contract(field.reshape(-1, width), vectors, ((1,), (1,)), HIGH)

    piece = piece.reshape(parts, groups // 2, 2, share * local_cols, RANK)
    own = jnp.where(low_bit == 0, piece[:, :, 0], piece[:, :, 1])
    other = exchanged(jnp.where(low_bit == 0, piece[:, :, 1], piece[:, :, 0]), 1)
    left = jnp.where(low_bit == 0, own, other)
    right = jnp.where(low_bit == 0, other, own)
    joined = jnp.concatenate([left, right], axis=3)
    kept = jnp.where(side == 0, joined[:, 0], joined[:, 1])
    arrived = exchanged(jnp.where(side == 0, joined[:, 1], joined[:, 0]), 2)
    gram = gram_of(left.reshape(-1, RANK), right.reshape(-1, RANK), padded_rows(2))
    vectors = vectors_of(summed(gram, 2, 1))
    far_vectors = exchanged(vectors, 2)

    kept = contract(kept.reshape(-1, 2 * RANK), vectors, ((1,), (1,)), HIGH)
    arrived = contract(arrived.reshape(-1, 2 * RANK), far_vectors, ((1,), (1,)), HIGH)
    left = jnp.where(side == 0, kept, arrived)
    right = jnp.where(side == 0, arrived, kept)
    gram = gram_of(left, right, padded_rows(4))
    vectors = vectors_of(summed(gram, 4, 2))
    basis = contract(vectors[:, :RANK], left, ((1,), (1,)), HIGH)
    basis = basis + contract(vectors[:, RANK:], right, ((1,), (1,)), HIGH)

    columns = RANK // groups
    basis = basis.reshape(groups, columns, -1)
    shares = [
        exchanged(lax.dynamic_index_in_dim(basis, mine ^ mask, 0, keepdims=False), mask)
        if mask
        else lax.dynamic_index_in_dim(basis, mine, 0, keepdims=False)
        for mask in range(groups)
    ]
    whole = jnp.stack(
        [
            lax.select_n(mine, *[shares[member ^ index] for index in range(groups)])
            for member in range(groups)
        ]
    )
    whole = whole.reshape(groups, columns, parts, share, local_cols)
    return whole.transpose(2, 0, 3, 4, 1).reshape(parts, local_rows, local_cols, columns)


def solution(mesh):
    return jax.shard_map(
        on_device,
        mesh=mesh,
        in_specs=(P(None, "gx", "gy", "cyc"),),
        out_specs=P(None, "gx", "gy", "cyc"),
        check_vma=False,
    )
```

time: 623 us -> 186 us (0.30)
  waiting for transfers between devices: 283 us -> 21.8 us
  other arithmetic: 233 us -> 4.89 us
  Pallas kernels: 0 us -> 128 us
  matrix products: 62 us -> 8.68 us
  between operations: 16.4 us -> 0.22 us
    another operation x46 -> x0, other arithmetic: 212 us -> none  [the longest x27 112 us: vectors_of(): lower = jnp.linalg.cholesky(gram_of(moved))]
    psum x3 -> x0, waiting for transfers between devices: 204 us -> none  [truncate(): return finish(joined, lax.psum(gram_of(joined), ('gx', 'gy')))]
    pallas_call x0 -> x9, Pallas kernels: none -> 128 us  [the longest x3 58.6 us: vectors_of(): pl.pallas_call(vectors_kernel, out_shape=jax.ShapeDtypeStruct((RANK, 2 *...]
    ppermute x6 -> x10, waiting for transfers between devices: 79.1 us -> 21.8 us  [the longest x6 17.1 us: exchanged(): return lax.ppermute(value, 'cyc', pairs)]
    dot_general x24 -> x5, matrix products: 59.2 us -> 8.68 us  [contract(): lax.dot_general(left, right, (dims, ((), ())), precision=precision, prefe...]
    ppermute x6 -> x10, starting transfers between devices: 12.5 us -> 14.9 us  [the longest x2 8.33 us: neighbours(): lax.ppermute(lax.slice_in_dim(block, size - 1, size, axis=dim), axis, for...]
  transfers between devices with their start and end apart: 9 -> 10, of which waited for: 9 -> 6; matrix products, arithmetic and copies ran while one was open for 1% -> 1% of each run, Pallas kernels for 0% -> 20%
where the time goes in v1:
time: 186 us; the launch traced here: 185 us
  Pallas kernels  128 us (69%)
  waiting for transfers between devices  21.8 us (12%)
  starting transfers between devices  14.9 us (8%)
  matrix products  8.68 us (5%)
  local copies, waits for them, and re-layouts  6.86 us (4%)
  other arithmetic  4.89 us (3%)
    pallas_call x3, Pallas kernels, vectors_of(): pl.pallas_call(vectors_kernel, out_shape=jax.ShapeDtypeStruct((RANK, 2 *...  58.6 us
    pallas_call x3, Pallas kernels, summed(): pl.pallas_call(functools.partial(sum_kernel, sizes), out_shape=jax.ShapeD...  51.8 us
    ppermute x6, waiting for transfers between devices, exchanged(): return lax.ppermute(value, 'cyc', pairs)  17.1 us
    pallas_call x1, Pallas kernels, strain(): pl.pallas_call(strain_kernel, grid=(rows,), in_specs=whole, out_specs=[pl...  14.3 us
    dot_general x5, matrix products, contract(): lax.dot_general(left, right, (dims, ((), ())), precision=precision, prefe...  8.68 us
    ppermute x2, starting transfers between devices, neighbours(): lax.ppermute(lax.slice_in_dim(block, size - 1, size, axis=dim), axis, for...  8.33 us
    ppermute x2, waiting for transfers between devices, neighbours(): high = lax.ppermute(lax.slice_in_dim(block, 0, 1, axis=dim), axis, backward)  4.25 us
    ppermute x6, starting transfers between devices, exchanged(): return lax.ppermute(value, 'cyc', pairs)  4.02 us
  transfers between devices with their start and end apart: 10, of which 6 were waited for; matrix products, arithmetic and copies ran while one was open for 1% of the time, Pallas kernels for 20%

profile of v1, /device:TPU:0, one launch (start us, length us, event | category | flops | bytes accessed | tf_op | source)
XLA Modules:
  0.0 185.4 jit_solution(9056916825073354663)
XLA Ops:
  0.0 1.0 fusion.12
  1.0 4.8 %collective-permute-start = (bf16[2,1,128,256]{3,2,1,0:T(8,128)(2,1)S(1)}, bf16[2,1,128,256]{3,2,1,0:T(8,128)(2,1)S(1)}, u32[]{:S(2)}, u32[]{:S(2)}) collective-permute-start(bf16[2,1,128,256]{3,2,1,0:T(8,128)(2,1)S(1)} %get-tuple-element.16), channel_id=1, source_target_pairs={{0,16},{1,17},{2,18},{3,19},{4,20},{5,21},{6,22},{7,23},{8,24},{9,... | collective-permute-start | bytes 393224 | tf_op jit(solution)/shard_map/ppermute | solution.py:24
  5.8 1.3 collective-permute-start.1
  7.1 1.1 fusion.11
  8.3 3.5 %collective-permute-start.2 = (bf16[2,24,1,256]{3,2,1,0:T(2,128)(2,1)S(1)}, bf16[2,24,1,256]{3,2,1,0:T(2,128)(2,1)S(1)}, u32[]{:S(2)}, u32[]{:S(2)}) collective-permute-start(bf16[2,24,1,256]{3,2,1,0:T(2,128)(2,1)S(1)} %get-tuple-element.14), channel_id=1, source_target_pairs={{0,4},{4,8},{8,12},{1,5},{5,9},{9,13},{2,6},{6,10},{10,14},{3,7},{... | collective-permute-start | bytes 73736 | tf_op jit(solution)/shard_map/ppermute | solution.py:24
  11.7 1.3 collective-permute-start.3
  13.1 0.4 collective-permute-done.2.ylo_ref
  13.5 4.3 %collective-permute-done.3.yhi_ref = bf16[2,24,1,256]{3,2,1,0:T(2,128)(2,1)S(1)} collective-permute-done((bf16[2,24,1,256]{3,2,1,0:T(2,128)(2,1)S(1)}, bf16[2,24,1,256]{3,2,1,0:T(2,128)(2,1)S(1)}, u32[]{:S(2)}, u32[]{:S(2)}) %collective-permute-start.3) | collective-permute-done | bytes 24608 | tf_op jit(solution)/shard_map/ppermute | solution.py:25
  17.7 0.0 collective-permute-done.xlo_ref
  17.7 0.0 collective-permute-done.1.xhi_ref
  17.7 1.9 %copy-done = bf16[2,24,128,256]{3,2,1,0:T(8,128)(2,1)S(1)} copy-done((bf16[2,24,128,256]{3,2,1,0:T(8,128)(2,1)S(1)}, bf16[2,24,128,256]{3,2,1,0:T(8,128)(2,1)}, u32[]{:S(2)}) %copy-start) | copy-done | bytes 3145752
  19.6 14.3 %shard_map.17 = (f32[2,24,128,256]{3,2,1,0:T(8,128)}, f32[384,128]{1,0:T(8,128)S(1)}) custom-call(bf16[2,24,128,256]{3,2,1,0:T(8,128)(2,1)S(1)} %copy-done, bf16[2,1,128,256]{3,2,1,0:T(8,128)(2,1)S(1)} %collective-permute-done.xlo_ref, bf16[2,1,128,256]{3,2,1,0:T(8,128)(2,1)S(1)} %collective-permute-done.1.xhi_ref, ...), custom_call_target="tpu_custom_call" | custom-call | tf_op jit(solution)/shard_map/pallas_call | solution.py:104
  34.0 16.2 %shard_map.18.gram_ref = f32[384,128]{1,0:T(8,128)S(1)} custom-call(f32[384,128]{1,0:T(8,128)S(1)} %get-tuple-element.8.x_ref), custom_call_target="tpu_custom_call" | custom-call | tf_op jit(solution)/shard_map/pallas_call | solution.py:230
  50.2 19.5 %shard_map.19 = f32[128,256]{1,0:T(8,128)S(1)} custom-call(f32[384,128]{1,0:T(8,128)S(1)} %shard_map.18.gram_ref), custom_call_target="tpu_custom_call" | custom-call | tf_op jit(solution)/shard_map/pallas_call | solution.py:308
  69.6 4.7 %fusion.6 = f32[2,2,2,768,128]{4,3,2,1,0:T(8,128)S(1)} fusion(f32[2,2,2,768,256]{4,3,2,1,0:T(8,128)} %bitcast.70, f32[128,256]{1,0:T(8,128)S(1)} %shard_map.19), kind=kOutput, calls=%fused_computation.26 | convolution fusion | flops 1207959552 | bytes 9568256 | tf_op jit(solution)/shard_map/dot_general | solution.py:35
  74.4 0.2 select_bitcast_fusion.1
  74.6 1.5 copy-done.1
  76.1 0.0 collective-permute-start.4
  76.1 3.5 %collective-permute-done.4 = f32[2,2,768,128]{3,2,1,0:T(8,128)} collective-permute-done((f32[2,2,768,128]{3,2,1,0:T(8,128)S(1)}, f32[2,2,768,128]{3,2,1,0:T(8,128)}, u32[]{:S(2)}, u32[]{:S(2)}) %collective-permute-start.4) | collective-permute-done | bytes 1572896 | tf_op jit(solution)/shard_map/ppermute | solution.py:31
  79.6 2.6 %broadcast_select_fusion.1 = (f32[2,2,768,128]{3,2,1,0:T(8,128)S(1)}, f32[2,2,768,128]{3,2,1,0:T(8,128)S(1)}) fusion(f32[2,2,768,128]{3,2,1,0:T(8,128)} %collective-permute-done.4, pred[]{:T(512)S(6)} %eq.5, f32[2,2,2,768,128]{4,3,2,1,0:T(8,128)} %copy-done.1), kind=kLoop, calls=%fused_computation.11 | loop fusion | flops 1179648 | bytes 7865344 | tf_op jit(solution)/shard_map/jit(_where)/select_n | solution.py:336
  82.2 1.9 %select_bitcast_fusion = (f32[2,768,256]{2,1,0:T(8,128)}, f32[2,1,768,256]{3,2,1,0:T(8,128)}) fusion(pred[]{:T(512)S(6)} %eq.4, f32[2,2,768,128]{3,2,1,0:T(8,128)S(1)} %get-tuple-element.10, f32[2,2,768,128]{3,2,1,0:T(8,128)S(1)} %get-tuple-element.9), kind=kLoop, calls=%fused_computation.7 | loop fusion | flops 1966080 | bytes 6291457 | tf_op jit(solution)/shard_map/jit(_where)/select_n | solution.py:340
  84.1 1.5 collective-permute-start.5
  85.6 2.2 %shard_map.20.x_ref = f32[384,128]{1,0:T(8,128)S(1)} custom-call(f32[3072,128]{1,0:T(8,128)S(1)} %bitcast.68, f32[3072,128]{1,0:T(8,128)S(1)} %bitcast.69), custom_call_target="tpu_custom_call" | custom-call | tf_op jit(solution)/shard_map/pallas_call | solution.py:140
  87.8 14.8 %shard_map.21.gram_ref = f32[384,128]{1,0:T(8,128)S(1)} custom-call(f32[384,128]{1,0:T(8,128)S(1)} %shard_map.20.x_ref), custom_call_target="tpu_custom_call" | custom-call | tf_op jit(solution)/shard_map/pallas_call | solution.py:230
  102.6 19.7 %shard_map.22 = f32[128,256]{1,0:T(8,128)S(1)} custom-call(f32[384,128]{1,0:T(8,128)S(1)} %shard_map.21.gram_ref), custom_call_target="tpu_custom_call" | custom-call | tf_op jit(solution)/shard_map/pallas_call | solution.py:308
  122.3 0.6 collective-permute-start.6
  122.8 0.8 fusion.13
  123.6 4.5 %collective-permute-done.6 = f32[128,256]{1,0:T(8,128)S(1)} collective-permute-done((f32[128,256]{1,0:T(8,128)S(1)}, f32[128,256]{1,0:T(8,128)S(1)}, u32[]{:S(2)}, u32[]{:S(2)}) %collective-permute-start.6) | collective-permute-done | bytes 131104 | tf_op jit(solution)/shard_map/ppermute | solution.py:31
  128.2 0.0 collective-permute-done.5
  128.2 2.2 %broadcast_select_fusion.3 = (f32[1536,128]{1,0:T(8,128)S(1)}, f32[1536,128]{1,0:T(8,128)S(1)}) fusion(f32[1536,128]{1,0:T(8,128)S(1)} %fusion.13, pred[]{:T(512)S(6)} %eq.4, f32[1536,256]{1,0:T(8,128)} %bitcast.12, f32[128,256]{1,0:T(8,128)S(1)} %collective-permute-done.6), kind=kOutput, calls=%fused_computation.13 | convolution fusion | flops 302383104 | bytes 4063233 | tf_op jit(solution)/shard_map/dot_general | solution.py:35
  130.4 1.2 shard_map.23.x_ref
  131.6 20.8 %shard_map.24.gram_ref = f32[512,128]{1,0:T(8,128)S(1)} custom-call(f32[512,128]{1,0:T(8,128)S(1)} %shard_map.23.x_ref), custom_call_target="tpu_custom_call" | custom-call | tf_op jit(solution)/shard_map/pallas_call | solution.py:230
  152.4 19.5 %shard_map.25 = f32[128,256]{1,0:T(8,128)S(1)} custom-call(f32[512,128]{1,0:T(8,128)S(1)} %shard_map.24.gram_ref), custom_call_target="tpu_custom_call" | custom-call | tf_op jit(solution)/shard_map/pallas_call | solution.py:308
  171.9 0.5 fusion.9
  172.3 0.5 convolution_add_fusion
  172.8 0.1 dynamic-slice_bitcast_fusion.1
  172.9 0.3 collective-permute-start.7
  173.2 0.9 collective-permute-start.8
  174.2 0.7 collective-permute-start.9
  174.8 6.1 %collective-permute-done.8 = f32[32,1536]{1,0:T(8,128)S(1)} collective-permute-done((f32[32,1536]{1,0:T(8,128)S(1)}, f32[32,1536]{1,0:T(8,128)S(1)}, u32[]{:S(2)}, u32[]{:S(2)}) %collective-permute-start.8) | collective-permute-done | bytes 196640 | tf_op jit(solution)/shard_map/ppermute | solution.py:31
  180.9 2.9 %collective-permute-done.9 = f32[32,1536]{1,0:T(8,128)S(1)} collective-permute-done((f32[32,1536]{1,0:T(8,128)S(1)}, f32[32,1536]{1,0:T(8,128)S(1)}, u32[]{:S(2)}, u32[]{:S(2)}) %collective-permute-start.9) | collective-permute-done | bytes 196640 | tf_op jit(solution)/shard_map/ppermute | solution.py:31
  183.8 0.1 fusion.2
  183.9 0.1 stack.15
  184.0 0.1 stack.16
  184.1 0.1 stack.17
  184.1 0.1 stack.18
  184.2 0.1 maximum_bitcast_fusion
  184.3 1.1 copy.14
  (5 shorter events, 0.0 us)
Async XLA Ops:
  1.0 16.7 %collective-permute-start = (bf16[2,1,128,256]{3,2,1,0:T(8,128)(2,1)S(1)}, bf16[2,1,128,256]{3,2,1,0:T(8,128)(2,1)S(1)}, u32[]{:S(2)}, u32[]{:S(2)}) collective-permute-start(bf16[2,1,128,256]{3,2,1,0:T(8,128)(2,1)S(1)} %get-tuple-element.16), channel_id=1, source_target_pairs={{0,16},{1,17},{2,18},{3,19},{4,20},{5,21},{6,22},{7,23},{8,24},{9,... | collective-permute-start | bytes 393224 | tf_op jit(solution)/shard_map/ppermute | solution.py:24
  5.8 11.9 %collective-permute-start.1 = (bf16[2,1,128,256]{3,2,1,0:T(8,128)(2,1)S(1)}, bf16[2,1,128,256]{3,2,1,0:T(8,128)(2,1)S(1)}, u32[]{:S(2)}, u32[]{:S(2)}) collective-permute-start(bf16[2,1,128,256]{3,2,1,0:T(8,128)(2,1)S(1)} %get-tuple-element.15), channel_id=1, source_target_pairs={{16,0},{17,1},{18,2},{19,3},{20,4},{21,5},{22,6},{23,7},{24,8},{25... | collective-permute-start | bytes 393224 | tf_op jit(solution)/shard_map/ppermute | solution.py:25
  8.3 5.2 %collective-permute-start.2 = (bf16[2,24,1,256]{3,2,1,0:T(2,128)(2,1)S(1)}, bf16[2,24,1,256]{3,2,1,0:T(2,128)(2,1)S(1)}, u32[]{:S(2)}, u32[]{:S(2)}) collective-permute-start(bf16[2,24,1,256]{3,2,1,0:T(2,128)(2,1)S(1)} %get-tuple-element.14), channel_id=1, source_target_pairs={{0,4},{4,8},{8,12},{1,5},{5,9},{9,13},{2,6},{6,10},{10,14},{3,7},{... | collective-permute-start | bytes 73736 | tf_op jit(solution)/shard_map/ppermute | solution.py:24
  11.7 6.0 %collective-permute-start.3 = (bf16[2,24,1,256]{3,2,1,0:T(2,128)(2,1)S(1)}, bf16[2,24,1,256]{3,2,1,0:T(2,128)(2,1)S(1)}, u32[]{:S(2)}, u32[]{:S(2)}) collective-permute-start(bf16[2,24,1,256]{3,2,1,0:T(2,128)(2,1)S(1)} %get-tuple-element.13), channel_id=1, source_target_pairs={{4,0},{8,4},{12,8},{5,1},{9,5},{13,9},{6,2},{10,6},{14,10},{7,3},{... | collective-permute-start | bytes 73736 | tf_op jit(solution)/shard_map/ppermute | solution.py:25
  17.7 1.9 %copy-start = (bf16[2,24,128,256]{3,2,1,0:T(8,128)(2,1)S(1)}, bf16[2,24,128,256]{3,2,1,0:T(8,128)(2,1)}, u32[]{:S(2)}) copy-start(bf16[2,24,128,256]{3,2,1,0:T(8,128)(2,1)} %u_ref.1) | copy-start | bytes 9437188
  74.4 1.7 copy-start.1
  76.1 3.5 %collective-permute-start.4 = (f32[2,2,768,128]{3,2,1,0:T(8,128)S(1)}, f32[2,2,768,128]{3,2,1,0:T(8,128)}, u32[]{:S(2)}, u32[]{:S(2)}) collective-permute-start(f32[2,2,768,128]{3,2,1,0:T(8,128)S(1)} %select_bitcast_fusion.1), channel_id=1, source_target_pairs={{0,1},{1,0},{2,3},{3,2},{4,5},{5,4},{6,7},{7,6},{8,9},{9,8},{10,11... | collective-permute-start | bytes 4718600 | tf_op jit(solution)/shard_map/ppermute | solution.py:31
  84.1 44.1 %collective-permute-start.5 = (f32[2,768,256]{2,1,0:T(8,128)}, f32[2,768,256]{2,1,0:T(8,128)}, u32[]{:S(2)}, u32[]{:S(2)}) collective-permute-start(f32[2,768,256]{2,1,0:T(8,128)} %get-tuple-element.11), channel_id=1, source_target_pairs={{0,2},{1,3},{2,0},{3,1},{4,6},{5,7},{6,4},{7,5},{8,10},{9,11},{10,... | collective-permute-start | bytes 4718600 | tf_op jit(solution)/shard_map/ppermute | solution.py:31
  85.6 37.2 %copy-start.2 = (f32[2,1,768,256]{3,2,1,0:T(8,128)S(1)}, f32[2,1,768,256]{3,2,1,0:T(8,128)}, u32[]{:S(2)}) copy-start(f32[2,1,768,256]{3,2,1,0:T(8,128)} %get-tuple-element.12) | copy-start | bytes 4718596
  122.3 5.9 %collective-permute-start.6 = (f32[128,256]{1,0:T(8,128)S(1)}, f32[128,256]{1,0:T(8,128)S(1)}, u32[]{:S(2)}, u32[]{:S(2)}) collective-permute-start(f32[128,256]{1,0:T(8,128)S(1)} %shard_map.22), channel_id=1, source_target_pairs={{0,2},{1,3},{2,0},{3,1},{4,6},{5,7},{6,4},{7,5},{8,10},{9,11},{10,... | collective-permute-start | bytes 393224 | tf_op jit(solution)/shard_map/ppermute | solution.py:31
  172.9 1.9 %collective-permute-start.7 = (f32[32,1536]{1,0:T(8,128)S(1)}, f32[32,1536]{1,0:T(8,128)S(1)}, u32[]{:S(2)}, u32[]{:S(2)}) collective-permute-start(f32[32,1536]{1,0:T(8,128)S(1)} %get-tuple-element.25), channel_id=1, source_target_pairs={{0,1},{1,0},{2,3},{3,2},{4,5},{5,4},{6,7},{7,6},{8,9},{9,8},{10,11... | collective-permute-start | bytes 589832 | tf_op jit(solution)/shard_map/ppermute | solution.py:31
  173.2 7.7 %collective-permute-start.8 = (f32[32,1536]{1,0:T(8,128)S(1)}, f32[32,1536]{1,0:T(8,128)S(1)}, u32[]{:S(2)}, u32[]{:S(2)}) collective-permute-start(f32[32,1536]{1,0:T(8,128)S(1)} %get-tuple-element.23), channel_id=1, source_target_pairs={{0,2},{1,3},{2,0},{3,1},{4,6},{5,7},{6,4},{7,5},{8,10},{9,11},{10,... | collective-permute-start | bytes 589832 | tf_op jit(solution)/shard_map/ppermute | solution.py:31
  174.2 9.7 %collective-permute-start.9 = (f32[32,1536]{1,0:T(8,128)S(1)}, f32[32,1536]{1,0:T(8,128)S(1)}, u32[]{:S(2)}, u32[]{:S(2)}) collective-permute-start(f32[32,1536]{1,0:T(8,128)S(1)} %get-tuple-element.24), channel_id=1, source_target_pairs={{0,3},{1,2},{2,1},{3,0},{4,7},{5,6},{6,5},{7,4},{8,11},{9,10},{10,... | collective-permute-start | bytes 589832 | tf_op jit(solution)/shard_map/ppermute | solution.py:31

commit v2 on v1

--- a/solution.py
+++ b/solution.py
@@ -16,14 +16,71 @@
 VMEM_LIMIT = 48 * 1024 * 1024
 
 
-def neighbours(block, axis, dim):
-    count = lax.axis_size(axis)
-    forward = [(i, i + 1) for i in range(count - 1)]
-    backward = [(target, source) for source, target in forward]
-    size = block.shape[dim]
-    low = lax.ppermute(lax.slice_in_dim(block, size - 1, size, axis=dim), axis, forward)
-    high = lax.ppermute(lax.slice_in_dim(block, 0, 1, axis=dim), axis, backward)
-    return low, high
+def halo_kernel(u_ref, top_ref, bottom_ref, xlo, xhi, ylo, yhi, send, recv):
+    rows = u_ref.shape[1]
+    sides = []
+    for axis, low, high, first, last in (
+        ("gx", xlo, xhi, u_ref.at[:, pl.ds(0, 1)], u_ref.at[:, pl.ds(rows - 1, 1)]),
+        ("gy", ylo, yhi, top_ref, bottom_ref),
+    ):
+        at = lax.axis_index(axis)
+        count = lax.axis_size(axis)
+        has_low = at > 0
+        has_high = at < count - 1
+        below = {axis: jnp.maximum(at - 1, 0)}
+        above = {axis: jnp.minimum(at + 1, count - 1)}
+        sides.append((below, has_low, first, high, has_high))
+        sides.append((above, has_high, last, low, has_low))
+
+    barrier = pltpu.get_barrier_semaphore()
+    for target, sends, *_ in sides:
+        @pl.when(sends)
+        def _():
+            pl.semaphore_signal(barrier, inc=1, device_id=target, device_id_type=MESH)
+    pl.semaphore_wait(barrier, sum(sends.astype(jnp.int32) for _, sends, *_ in sides))
+
+    def copy(index):
+        target, _, source, landing, _ = sides[index]
+        return pltpu.make_async_remote_copy(
+            src_ref=source, dst_ref=landing, send_sem=send.at[index], recv_sem=recv.at[index],
+            device_id=target, device_id_type=MESH,
+        )
+
+    for index, (_, sends, _, landing, receives) in enumerate(sides):
+        @pl.when(sends)
+        def _():
+            copy(index).start()
+
+        @pl.when(jnp.logical_not(receives))
+        def _():
+            landing[...] = jnp.zeros_like(landing)
+    for index, (_, sends, _, _, receives) in enumerate(sides):
+        @pl.when(sends)
+        def _():
+            copy(index).wait_send()
+
+        @pl.when(receives)
+        def _():
+            copy(index).wait_recv()
+
+
+def halo_of(u):
+    parts, rows, cols, width = u.shape
+    top = u[:, :, 0].astype(jnp.float32).reshape(parts * rows, width)
+    bottom = u[:, :, cols - 1].astype(jnp.float32).reshape(parts * rows, width)
+    across = jax.ShapeDtypeStruct((parts, 1, cols, width), u.dtype)
+    along = jax.ShapeDtypeStruct(top.shape, jnp.float32)
+    vmem = pl.BlockSpec(memory_space=pltpu.VMEM)
+    return pl.pallas_call(
+        halo_kernel,
+        out_shape=[across, across, along, along],
+        in_specs=[pl.BlockSpec(memory_space=pl.ANY), vmem, vmem],
+        out_specs=[vmem] * 4,
+        scratch_shapes=[pltpu.SemaphoreType.DMA((4,))] * 2,
+        compiler_params=pltpu.CompilerParams(
+            collective_id=3, has_side_effects=True, vmem_limit_bytes=VMEM_LIMIT
+        ),
+    )(u, top, bottom)
 
 
 def exchanged(value, mask):
@@ -58,7 +115,7 @@
 
 def strain_kernel(u_ref, xlo_ref, xhi_ref, ylo_ref, yhi_ref, f_ref, gram_ref, main, cross):
     i = pl.program_id(0)
-    rows = pl.num_programs(0)
+    rows = u_ref.shape[1]
     cols = u_ref.shape[2]
 
     @pl.when(i == 0)
@@ -79,8 +136,8 @@
         here = u_ref[part, i].astype(jnp.float32)
         before = pltpu.roll(here, 1, 0)
         after = pltpu.roll(here, cols - 1, 0)
-        before = jnp.where(node == 0, ylo_ref[part, i].astype(jnp.float32), before)
-        after = jnp.where(node == cols - 1, yhi_ref[part, i].astype(jnp.float32), after)
+        before = jnp.where(node == 0, ylo_ref[pl.ds(part * rows + i, 1), :], before)
+        after = jnp.where(node == cols - 1, yhi_ref[pl.ds(part * rows + i, 1), :], after)
         return (after - before) * 0.5
 
     exx = dx(0)
@@ -100,7 +157,7 @@
 
 def strain(u, halo, padded):
     parts, rows, cols, width = u.shape
-    whole = [pl.BlockSpec(a.shape, lambda i: (0, 0, 0, 0)) for a in (u, *halo)]
+    whole = [pl.BlockSpec(a.shape, lambda i, rank=a.ndim: (0,) * rank) for a in (u, *halo)]
     return pl.pallas_call(
         strain_kernel,
         grid=(rows,),
@@ -118,32 +175,33 @@
     )(u, *halo)
 
 
-def gram_kernel(left_ref, right_ref, gram_ref, main, cross):
+def cross_kernel(left_ref, right_ref, gram_ref):
     step = pl.program_id(0)
 
     @pl.when(step == 0)
     def _():
-        main[...] = jnp.zeros_like(main)
-        cross[...] = jnp.zeros_like(cross)
-
-    add_gram(main, cross, jnp.concatenate([left_ref[...], right_ref[...]], axis=1))
-
-    @pl.when(step == pl.num_programs(0) - 1)
-    def _():
-        upper_blocks(gram_ref, main[...] + cross[...] + cross[...].T)
-
-
-def gram_of(left, right, padded):
+        gram_ref[...] = jnp.zeros_like(gram_ref)
+
+    left_high, left_low = split(left_ref[...])
+    right_high, right_low = split(right_ref[...])
+    rows = ((0,), (0,))
+    gram_ref[:RANK] += (
+        contract(left_high, right_high, rows)
+        + contract(left_high, right_low, rows)
+        + contract(left_low, right_high, rows)
+    )
+
+
+def cross_of(left, right, padded):
     rows = left.shape[0]
     tile = 512 if rows % 512 == 0 else rows
     spec = pl.BlockSpec((tile, RANK), lambda i: (i, 0))
     return pl.pallas_call(
-        gram_kernel,
+        cross_kernel,
         grid=(rows // tile,),
         in_specs=[spec, spec],
         out_specs=pl.BlockSpec((padded, RANK), lambda i: (0, 0)),
         out_shape=jax.ShapeDtypeStruct((padded, RANK), jnp.float32),
-        scratch_shapes=[pltpu.VMEM((2 * RANK, 2 * RANK), jnp.float32)] * 2,
         compiler_params=pltpu.CompilerParams(vmem_limit_bytes=VMEM_LIMIT),
     )(left, right)
 
@@ -217,9 +275,9 @@
     return lax.axis_size("gx") * lax.axis_size("gy") * near
 
 
-def padded_rows(near):
+def padded_rows(near, blocks):
     n = group_size(near)
-    chunk = -(-3 * RANK // (8 * n)) * 8
+    chunk = -(-blocks * RANK // (8 * n)) * 8
     return n * chunk
 
 
@@ -241,32 +299,36 @@
 
 
 def eliminate(work):
-    parts = work.shape[1] // RANK
+    def row_of(value, index):
+        return value[index : index + 1, :]
+
     for start in range(0, RANK, PANEL):
-        rows = [
-            [work[start + i : start + i + 1, p * RANK : (p + 1) * RANK] for p in range(parts)]
-            for i in range(PANEL)
+        after = start + PANEL
+        rest = work[start:after, :]
+        columns = [
+            jnp.broadcast_to(work[start:after, start + k : start + k + 1], (PANEL, RANK))
+            for k in range(PANEL)
         ]
-        block = [
-            [
-                jnp.broadcast_to(
-                    work[start + i : start + i + 1, start + j : start + j + 1], (1, RANK)
-                )
-                for j in range(i + 1)
-            ]
-            for i in range(PANEL)
-        ]
-        for j in range(PANEL):
-            scale = lax.rsqrt(block[j][j])
-            rows[j] = [part * scale for part in rows[j]]
-            column = {i: block[i][j] * scale for i in range(j + 1, PANEL)}
-            for i in range(j + 1, PANEL):
-                for k in range(j + 1, i + 1):
-                    block[i][k] = block[i][k] - column[i] * column[k]
-                rows[i] = [part - column[i] * top for part, top in zip(rows[i], rows[j])]
-            for p in range(parts):
-                work[start + j : start + j + 1, p * RANK : (p + 1) * RANK] = rows[j][p]
-        after = start + PANEL
+        wide = lambda value: jnp.concatenate([value] * (rest.shape[1] // RANK), axis=1)
+        for j in range(0, PANEL, 2):
+            one = row_of(columns[j], j)
+            mixed = row_of(columns[j], j + 1)
+            two = row_of(columns[j + 1], j + 1)
+            root = lax.rsqrt(one)
+            second = lax.rsqrt(one * two - mixed * mixed) * (one * root)
+            lower = mixed * root
+            left = columns[j] * root
+            right = (columns[j + 1] - left * lower) * second
+            top = row_of(rest, j) * wide(root)
+            bottom = (row_of(rest, j + 1) - top * wide(lower)) * wide(second)
+            work[start + j : start + j + 1, :] = top
+            work[start + j + 1 : start + j + 2, :] = bottom
+            if j + 2 < PANEL:
+                for k in range(j + 2, PANEL):
+                    columns[k] = columns[k] - (
+                        left * row_of(left, k) + right * row_of(right, k)
+                    )
+                rest = rest - (wide(left) * top + wide(right) * bottom)
         if after < RANK:
             panel = work[start:after, :]
             work[after:, :] = work[after:, :] - contract(
@@ -274,16 +336,17 @@
             )
 
 
-def vectors_kernel(gram_ref, v_ref, normed, work):
+def vectors_kernel(first_ref, cross_ref, last_ref, v_ref, own_ref, normed, work):
     width = 2 * RANK
-    first = gram_ref[0:RANK]
-    cross = gram_ref[RANK : 2 * RANK]
-    last = gram_ref[2 * RANK : 3 * RANK]
+    first = first_ref[...]
+    cross = cross_ref[...]
+    last = last_ref[...]
     row = lax.broadcasted_iota(jnp.int32, (RANK, RANK), 0)
     col = lax.broadcasted_iota(jnp.int32, (RANK, RANK), 1)
     diagonal = jnp.where(row == col, first + last, 0.0)
     trace = jnp.sum(jnp.sum(diagonal, axis=0, keepdims=True), axis=1, keepdims=True)
-    scale = 1.0 / (trace / width + 1e-06)
+    level = trace / width + 1e-06
+    scale = 1.0 / level
     normed[:RANK, :RANK] = first * scale
     normed[:RANK, RANK:] = cross * scale
     normed[RANK:, :RANK] = (cross * scale).T
@@ -296,26 +359,42 @@
             work[:, RANK:] = contract(work[:, RANK:], normed[...], ((1,), (0,)), HIGHEST)
 
         moved = work[:, RANK:]
-        work[:, :RANK] = contract(moved, moved, ((1,), (1,)), HIGHEST)
+        gram = contract(moved, moved, ((1,), (1,)), HIGHEST)
+        kept = jnp.where(row == col, gram, 0.0)
+        down = lax.rsqrt(jnp.sum(kept, axis=1, keepdims=True))
+        along = lax.rsqrt(jnp.sum(kept, axis=0, keepdims=True))
+        work[:, :RANK] = gram * down * along
+        work[:, RANK:] = moved * down
         eliminate(work)
         return carry
 
     lax.fori_loop(0, POWER, step, 0)
-    v_ref[...] = work[:, RANK:]
-
-
-def vectors_of(gram):
+    vectors = work[:, RANK:]
+    v_ref[...] = vectors
+    moved = contract(vectors, normed[...], ((1,), (0,)), HIGHEST)
+    own_ref[...] = contract(moved, vectors, ((1,), (1,)), HIGHEST) * level
+
+
+def vectors_of(*blocks):
+    tile = (RANK, RANK)
     return pl.pallas_call(
         vectors_kernel,
-        out_shape=jax.ShapeDtypeStruct((RANK, 2 * RANK), jnp.float32),
-        in_specs=[pl.BlockSpec(memory_space=pltpu.VMEM)],
-        out_specs=pl.BlockSpec(memory_space=pltpu.VMEM),
+        grid=(1,),
+        out_shape=[
+            jax.ShapeDtypeStruct((RANK, 2 * RANK), jnp.float32),
+            jax.ShapeDtypeStruct(tile, jnp.float32),
+        ],
+        in_specs=[pl.BlockSpec(tile, lambda i, at=at: (at, 0)) for _, at in blocks],
+        out_specs=[
+            pl.BlockSpec((RANK, 2 * RANK), lambda i: (0, 0)),
+            pl.BlockSpec(tile, lambda i: (0, 0)),
+        ],
         scratch_shapes=[
             pltpu.VMEM((2 * RANK, 2 * RANK), jnp.float32),
             pltpu.VMEM((RANK, 3 * RANK), jnp.float32),
         ],
         compiler_params=pltpu.CompilerParams(vmem_limit_bytes=VMEM_LIMIT),
-    )(gram)
+    )(*[array for array, _ in blocks])
 
 
 def on_device(displacement):
@@ -325,9 +404,10 @@
     side = mine >> 1
     parts, local_rows, local_cols, width = displacement.shape
     share = local_rows // groups
-    halo = neighbours(displacement, "gx", 1) + neighbours(displacement, "gy", 2)
-    field, gram = strain(displacement, halo, padded_rows(1))
-    vectors = vectors_of(summed(gram, 1, 0))
+    field, gram = strain(displacement, halo_of(displacement), padded_rows(1, 3))
+    gram = summed(gram, 1, 0)
+    vectors, own_gram = vectors_of((gram, 0), (gram, 1), (gram, 2))
+    other_gram = exchanged(own_gram, 1)
     piece = contract(field.reshape(-1, width), vectors, ((1,), (1,)), HIGH)
 
     piece = piece.reshape(parts, groups // 2, 2, share * local_cols, RANK)
@@ -338,16 +418,21 @@
     joined = jnp.concatenate([left, right], axis=3)
     kept = jnp.where(side == 0, joined[:, 0], joined[:, 1])
     arrived = exchanged(jnp.where(side == 0, joined[:, 1], joined[:, 0]), 2)
-    gram = gram_of(left.reshape(-1, RANK), right.reshape(-1, RANK), padded_rows(2))
-    vectors = vectors_of(summed(gram, 2, 1))
-    far_vectors = exchanged(vectors, 2)
+    cross = cross_of(left.reshape(-1, RANK), right.reshape(-1, RANK), padded_rows(2, 1))
+    first = jnp.where(low_bit == 0, own_gram, other_gram)
+    last = jnp.where(low_bit == 0, other_gram, own_gram)
+    vectors, own_gram = vectors_of((first, 0), (summed(cross, 2, 1), 0), (last, 0))
+    far = exchanged(jnp.concatenate([vectors, own_gram], axis=1), 2)
+    far_vectors, far_gram = far[:, : 2 * RANK], far[:, 2 * RANK :]
 
     kept = contract(kept.reshape(-1, 2 * RANK), vectors, ((1,), (1,)), HIGH)
     arrived = contract(arrived.reshape(-1, 2 * RANK), far_vectors, ((1,), (1,)), HIGH)
     left = jnp.where(side == 0, kept, arrived)
     right = jnp.where(side == 0, arrived, kept)
-    gram = gram_of(left, right, padded_rows(4))
-    vectors = vectors_of(summed(gram, 4, 2))
+    cross = cross_of(left, right, padded_rows(4, 1))
+    first = jnp.where(side == 0, own_gram, far_gram)
+    last = jnp.where(side == 0, far_gram, own_gram)
+    vectors, _ = vectors_of((first, 0), (summed(cross, 4, 2), 0), (last, 0))
     basis = contract(vectors[:, :RANK], left, ((1,), (1,)), HIGH)
     basis = basis + contract(vectors[:, RANK:], right, ((1,), (1,)), HIGH)
 

time: 186 us -> 159 us (0.85)
  Pallas kernels: 128 us -> 112 us
  starting transfers between devices: 14.9 us -> 4.04 us
    pallas_call x3, Pallas kernels: 51.8 us -> 40.8 us  [summed(): pl.pallas_call(functools.partial(sum_kernel, sizes), out_shape=jax.ShapeD...]
    ppermute x4 -> x0, starting transfers between devices: 10.9 us -> none  [the longest x2 8.33 us: neighbours(): lax.ppermute(lax.slice_in_dim(block, size - 1, size, axis=dim), axis, for...]
    ppermute x6 -> x7, waiting for transfers between devices: 17.1 us -> 22.4 us  [exchanged(): return lax.ppermute(value, 'cyc', pairs)]
    ppermute x4 -> x0, waiting for transfers between devices: 4.68 us -> none  [the longest x2 4.25 us: neighbours(): high = lax.ppermute(lax.slice_in_dim(block, 0, 1, axis=dim), axis, backward)]
    pallas_call x5 -> x6, Pallas kernels: 62 us -> 57.3 us  [the longest x3 46.6 us: vectors_of(): pl.pallas_call(vectors_kernel, grid=(1,), out_shape=[jax.ShapeDtypeStruct...]
    ppermute x6 -> x7, starting transfers between devices: 4.02 us -> 4.04 us  [exchanged(): return lax.ppermute(value, 'cyc', pairs)]
  transfers between devices with their start and end apart: 10 -> 7, of which waited for: 6 -> 5; matrix products, arithmetic and copies ran while one was open for 1% -> 1% of each run, Pallas kernels for 20% -> 18%
where the time goes in v2:
time: 159 us
  Pallas kernels  112 us (70%)
  waiting for transfers between devices  22.4 us (14%)
  matrix products  8.69 us (5%)
  other arithmetic  6.23 us (4%)
  local copies, waits for them, and re-layouts  5.04 us (3%)
  starting transfers between devices  4.04 us (3%)
    pallas_call x3, Pallas kernels, vectors_of(): pl.pallas_call(vectors_kernel, grid=(1,), out_shape=[jax.ShapeDtypeStruct...  46.6 us
    pallas_call x3, Pallas kernels, summed(): pl.pallas_call(functools.partial(sum_kernel, sizes), out_shape=jax.ShapeD...  40.8 us
    ppermute x7, waiting for transfers between devices, exchanged(): return lax.ppermute(value, 'cyc', pairs)  22.4 us
    pallas_call x1, Pallas kernels, strain(): pl.pallas_call(strain_kernel, grid=(rows,), in_specs=whole, out_specs=[pl...  14.2 us
    dot_general x5, matrix products, contract(): lax.dot_general(left, right, (dims, ((), ())), precision=precision, prefe...  8.69 us
    pallas_call x1, Pallas kernels, halo_of(): pl.pallas_call(halo_kernel, out_shape=[across, across, along, along], in_...  7.8 us
    ppermute x7, starting transfers between devices, exchanged(): return lax.ppermute(value, 'cyc', pairs)  4.04 us
  transfers between devices with their start and end apart: 7, of which 5 were waited for; matrix products, arithmetic and copies ran while one was open for 1% of the time, Pallas kernels for 18%

profile of v2, /device:TPU:0, one launch (start us, length us, event | category | flops | bytes accessed | tf_op | source)
XLA Modules:
  0.0 158.9 jit_solution(5854048171582143149)
XLA Ops:
  0.0 1.1 fusion.13
  1.2 0.0 copy-start
  1.2 1.9 %copy-done = bf16[2,24,128,256]{3,2,1,0:T(8,128)(2,1)S(1)} copy-done((bf16[2,24,128,256]{3,2,1,0:T(8,128)(2,1)S(1)}, bf16[2,24,128,256]{3,2,1,0:T(8,128)(2,1)}, u32[]{:S(2)}) %copy-start) | copy-done | bytes 3145752
  3.1 7.8 %shard_map.17 = (bf16[2,1,128,256]{3,2,1,0:T(8,128)(2,1)S(1)}, bf16[2,1,128,256]{3,2,1,0:T(8,128)(2,1)S(1)}, f32[48,256]{1,0:T(8,128)S(1)}, f32[48,256]{1,0:T(8,128)S(1)}) custom-call(bf16[2,24,128,256]{3,2,1,0:T(8,128)(2,1)S(1)} %copy-done, f32[48,256]{1,0:T(8,128)S(1)} %get-tuple-element.47.top_ref, f32[48,256]{1,0:T(8,128)S(1)} %get-tuple-element.46.bottom_ref), custom_call_target="tpu_custom_call" | custom-call | tf_op jit(solution)/shard_map/pallas_call | solution.py:74
  10.9 14.2 %shard_map.18 = (f32[2,24,128,256]{3,2,1,0:T(8,128)}, f32[384,128]{1,0:T(8,128)S(1)}) custom-call(bf16[2,24,128,256]{3,2,1,0:T(8,128)(2,1)S(1)} %copy-done, bf16[2,1,128,256]{3,2,1,0:T(8,128)(2,1)S(1)} %get-tuple-element.16.xlo_ref, bf16[2,1,128,256]{3,2,1,0:T(8,128)(2,1)S(1)} %get-tuple-element.17.xhi_ref, f32[48,256]{1,0:T(8,128)S(1)} %get-tuple-element.18.ylo_ref, ...), custom_call_target="tpu_custom_call" | custom-call | tf_op jit(solution)/shard_map/pallas_call | solution.py:161
  25.0 14.0 %shard_map.19.first_ref.cross_ref.last_ref = f32[384,128]{1,0:T(8,128)S(1)} custom-call(f32[384,128]{1,0:T(8,128)S(1)} %get-tuple-element.20.x_ref), custom_call_target="tpu_custom_call" | custom-call | tf_op jit(solution)/shard_map/pallas_call | solution.py:288
  39.1 15.3 %shard_map.20 = (f32[128,256]{1,0:T(8,128)S(1)}, f32[128,128]{1,0:T(8,128)S(1)}) custom-call(f32[384,128]{1,0:T(8,128)S(1)} %shard_map.19.first_ref.cross_ref.last_ref, f32[384,128]{1,0:T(8,128)S(1)} %shard_map.19.first_ref.cross_ref.last_ref, f32[384,128]{1,0:T(8,128)S(1)} %shard_map.19.first_ref.cross_ref.last_ref), custom_call_target="tpu_custom_call" | custom-call | tf_op jit(solution)/shard_map/pallas_call | solution.py:380
  54.4 4.7 %fusion.8 = f32[2,2,2,768,128]{4,3,2,1,0:T(8,128)S(1)} fusion(f32[2,2,2,768,256]{4,3,2,1,0:T(8,128)} %bitcast.75, f32[128,256]{1,0:T(8,128)S(1)} %get-tuple-element.23), kind=kOutput, calls=%fused_computation.29 | convolution fusion | flops 1207959552 | bytes 9568256 | tf_op jit(solution)/shard_map/dot_general | solution.py:92
  59.1 0.0 copy-start.1
  59.1 1.5 select_bitcast_fusion.1
  60.6 0.6 copy-done.1
  61.2 0.0 collective-permute-start.1
  61.2 3.7 %collective-permute-done.1 = f32[2,2,768,128]{3,2,1,0:T(8,128)} collective-permute-done((f32[2,2,768,128]{3,2,1,0:T(8,128)}, f32[2,2,768,128]{3,2,1,0:T(8,128)}, u32[]{:S(2)}, u32[]{:S(2)}) %collective-permute-start.1) | collective-permute-done | bytes 1572896 | tf_op jit(solution)/shard_map/ppermute | solution.py:88
  65.0 2.6 %broadcast_select_fusion.2 = (f32[2,2,768,128]{3,2,1,0:T(8,128)S(1)}, f32[2,2,768,128]{3,2,1,0:T(8,128)S(1)}) fusion(f32[2,2,768,128]{3,2,1,0:T(8,128)} %collective-permute-done.1, pred[]{:T(512)S(6)} %eq.5, f32[2,2,2,768,128]{4,3,2,1,0:T(8,128)} %copy-done.1), kind=kLoop, calls=%fused_computation.12 | loop fusion | flops 1179648 | bytes 7865344 | tf_op jit(solution)/shard_map/jit(_where)/select_n | solution.py:416
  67.6 1.9 %select_bitcast_fusion = (f32[2,768,256]{2,1,0:T(8,128)}, f32[2,1,768,256]{3,2,1,0:T(8,128)}) fusion(pred[]{:T(512)S(6)} %eq.4, f32[2,2,768,128]{3,2,1,0:T(8,128)S(1)} %get-tuple-element.28, f32[2,2,768,128]{3,2,1,0:T(8,128)S(1)} %get-tuple-element.27), kind=kLoop, calls=%fused_computation.7 | loop fusion | flops 1966080 | bytes 6291457 | tf_op jit(solution)/shard_map/jit(_where)/select_n | solution.py:420
  69.5 1.5 collective-permute-start.3
  71.0 0.0 collective-permute-start
  71.0 1.3 collective-permute-done
  72.3 0.0 copy-start.2
  72.3 1.9 %shard_map.21.x_ref = f32[128,128]{1,0:T(8,128)S(1)} custom-call(f32[3072,128]{1,0:T(8,128)S(1)} %bitcast.73, f32[3072,128]{1,0:T(8,128)S(1)} %bitcast.74), custom_call_target="tpu_custom_call" | custom-call | tf_op jit(solution)/shard_map/pallas_call | solution.py:199
  74.2 11.2 %shard_map.22.cross_ref = f32[128,128]{1,0:T(8,128)S(1)} custom-call(f32[128,128]{1,0:T(8,128)S(1)} %shard_map.21.x_ref), custom_call_target="tpu_custom_call" | custom-call | tf_op jit(solution)/shard_map/pallas_call | solution.py:288
  85.5 15.3 %shard_map.23 = (f32[128,256]{1,0:T(8,128)S(1)}, f32[128,128]{1,0:T(8,128)S(1)}) custom-call(f32[128,128]{1,0:T(8,128)S(1)} %get-tuple-element.45.first_ref, f32[128,128]{1,0:T(8,128)S(1)} %shard_map.22.cross_ref, f32[128,128]{1,0:T(8,128)S(1)} %get-tuple-element.44.last_ref), custom_call_target="tpu_custom_call" | custom-call | tf_op jit(solution)/shard_map/pallas_call | solution.py:380
  100.8 0.6 collective-permute-start.2
  101.3 0.0 copy-done.2
  101.3 0.8 fusion.14
  102.1 8.2 %collective-permute-done.2 = f32[128,384]{1,0:T(8,128)S(1)} collective-permute-done((f32[128,384]{1,0:T(8,128)S(1)}, f32[128,384]{1,0:T(8,128)S(1)}, u32[]{:S(2)}, u32[]{:S(2)}) %collective-permute-start.2) | collective-permute-done | bytes 196640 | tf_op jit(solution)/shard_map/ppermute | solution.py:88
  110.4 0.0 collective-permute-done.3
  110.4 2.2 %broadcast_select_fusion.3 = (f32[1536,128]{1,0:T(8,128)S(1)}, f32[1536,128]{1,0:T(8,128)S(1)}) fusion(f32[1536,128]{1,0:T(8,128)S(1)} %fusion.14, pred[]{:T(512)S(6)} %eq.4, f32[1536,256]{1,0:T(8,128)} %bitcast.14, f32[128,384]{1,0:T(8,128)S(1)} %collective-permute-done.2), kind=kOutput, calls=%fused_computation.13 | convolution fusion | flops 302383104 | bytes 4063233 | tf_op jit(solution)/shard_map/dot_general | solution.py:92
  112.6 1.0 shard_map.24.x_ref
  113.6 15.5 %shard_map.25.cross_ref = f32[256,128]{1,0:T(8,128)S(1)} custom-call(f32[256,128]{1,0:T(8,128)S(1)} %shard_map.24.x_ref), custom_call_target="tpu_custom_call" | custom-call | tf_op jit(solution)/shard_map/pallas_call | solution.py:288
  129.1 16.1 %shard_map.26 = (f32[128,256]{1,0:T(8,128)S(1)}, f32[128,128]{1,0:T(8,128)}) custom-call(f32[128,128]{1,0:T(8,128)S(1)} %get-tuple-element.43.first_ref, f32[256,128]{1,0:T(8,128)S(1)} %shard_map.25.cross_ref, f32[128,128]{1,0:T(8,128)S(1)} %get-tuple-element.42.last_ref), custom_call_target="tpu_custom_call" | custom-call | tf_op jit(solution)/shard_map/pallas_call | solution.py:380
  145.2 0.5 fusion.11
  145.7 0.5 convolution_add_fusion
  146.1 0.1 dynamic-slice_bitcast_fusion.1
  146.2 0.2 collective-permute-start.4
  146.4 0.9 collective-permute-start.5
  147.3 0.8 collective-permute-start.6
  148.2 0.0 collective-permute-done.4
  148.2 5.9 %collective-permute-done.5 = f32[32,1536]{1,0:T(8,128)S(1)} collective-permute-done((f32[32,1536]{1,0:T(8,128)S(1)}, f32[32,1536]{1,0:T(8,128)S(1)}, u32[]{:S(2)}, u32[]{:S(2)}) %collective-permute-start.5) | collective-permute-done | bytes 196640 | tf_op jit(solution)/shard_map/ppermute | solution.py:88
  154.1 3.3 %collective-permute-done.6 = f32[32,1536]{1,0:T(8,128)S(1)} collective-permute-done((f32[32,1536]{1,0:T(8,128)S(1)}, f32[32,1536]{1,0:T(8,128)S(1)}, u32[]{:S(2)}, u32[]{:S(2)}) %collective-permute-start.6) | collective-permute-done | bytes 196640 | tf_op jit(solution)/shard_map/ppermute | solution.py:88
  157.3 0.1 fusion.2
  157.5 0.1 stack.15
  157.5 0.1 stack.16
  157.6 0.1 stack.17
  157.6 0.1 stack.18
  157.7 0.1 maximum_bitcast_fusion
  157.8 1.1 copy.18
  (6 shorter events, 0.1 us)
Async XLA Ops:
  1.2 1.9 %copy-start = (bf16[2,24,128,256]{3,2,1,0:T(8,128)(2,1)S(1)}, bf16[2,24,128,256]{3,2,1,0:T(8,128)(2,1)}, u32[]{:S(2)}) copy-start(bf16[2,24,128,256]{3,2,1,0:T(8,128)(2,1)} %u_ref.3) | copy-start | bytes 9437188
  59.1 2.1 %copy-start.1 = (f32[2,2,2,768,128]{4,3,2,1,0:T(8,128)}, f32[2,2,2,768,128]{4,3,2,1,0:T(8,128)S(1)}, u32[]{:S(2)}) copy-start(f32[2,2,2,768,128]{4,3,2,1,0:T(8,128)S(1)} %fusion.8) | copy-start | bytes 9437188
  61.2 3.8 %collective-permute-start.1 = (f32[2,2,768,128]{3,2,1,0:T(8,128)}, f32[2,2,768,128]{3,2,1,0:T(8,128)}, u32[]{:S(2)}, u32[]{:S(2)}) collective-permute-start(f32[2,2,768,128]{3,2,1,0:T(8,128)} %select_bitcast_fusion.1), channel_id=1, source_target_pairs={{0,1},{1,0},{2,3},{3,2},{4,5},{5,4},{6,7},{7,6},{8,9},{9,8},{10,11... | collective-permute-start | bytes 4718600 | tf_op jit(solution)/shard_map/ppermute | solution.py:88
  69.5 40.9 %collective-permute-start.3 = (f32[2,768,256]{2,1,0:T(8,128)}, f32[2,768,256]{2,1,0:T(8,128)}, u32[]{:S(2)}, u32[]{:S(2)}) collective-permute-start(f32[2,768,256]{2,1,0:T(8,128)} %get-tuple-element.29), channel_id=1, source_target_pairs={{0,2},{1,3},{2,0},{3,1},{4,6},{5,7},{6,4},{7,5},{8,10},{9,11},{10,... | collective-permute-start | bytes 4718600 | tf_op jit(solution)/shard_map/ppermute | solution.py:88
  71.0 1.3 collective-permute-start
  72.3 29.0 %copy-start.2 = (f32[2,1,768,256]{3,2,1,0:T(8,128)S(1)}, f32[2,1,768,256]{3,2,1,0:T(8,128)}, u32[]{:S(2)}) copy-start(f32[2,1,768,256]{3,2,1,0:T(8,128)} %get-tuple-element.30) | copy-start | bytes 4718596
  100.8 9.6 %collective-permute-start.2 = (f32[128,384]{1,0:T(8,128)S(1)}, f32[128,384]{1,0:T(8,128)S(1)}, u32[]{:S(2)}, u32[]{:S(2)}) collective-permute-start(f32[128,384]{1,0:T(8,128)S(1)} %pad_maximum_fusion.1), channel_id=1, source_target_pairs={{0,2},{1,3},{2,0},{3,1},{4,6},{5,7},{6,4},{7,5},{8,10},{9,11},{10,... | collective-permute-start | bytes 589832 | tf_op jit(solution)/shard_map/ppermute | solution.py:88
  146.2 2.0 %collective-permute-start.4 = (f32[32,1536]{1,0:T(8,128)S(1)}, f32[32,1536]{1,0:T(8,128)S(1)}, u32[]{:S(2)}, u32[]{:S(2)}) collective-permute-start(f32[32,1536]{1,0:T(8,128)S(1)} %get-tuple-element.41), channel_id=1, source_target_pairs={{0,1},{1,0},{2,3},{3,2},{4,5},{5,4},{6,7},{7,6},{8,9},{9,8},{10,11... | collective-permute-start | bytes 589832 | tf_op jit(solution)/shard_map/ppermute | solution.py:88
  146.4 7.7 %collective-permute-start.5 = (f32[32,1536]{1,0:T(8,128)S(1)}, f32[32,1536]{1,0:T(8,128)S(1)}, u32[]{:S(2)}, u32[]{:S(2)}) collective-permute-start(f32[32,1536]{1,0:T(8,128)S(1)} %get-tuple-element.39), channel_id=1, source_target_pairs={{0,2},{1,3},{2,0},{3,1},{4,6},{5,7},{6,4},{7,5},{8,10},{9,11},{10,... | collective-permute-start | bytes 589832 | tf_op jit(solution)/shard_map/ppermute | solution.py:88
  147.3 10.0 %collective-permute-start.6 = (f32[32,1536]{1,0:T(8,128)S(1)}, f32[32,1536]{1,0:T(8,128)S(1)}, u32[]{:S(2)}, u32[]{:S(2)}) collective-permute-start(f32[32,1536]{1,0:T(8,128)S(1)} %get-tuple-element.40), channel_id=1, source_target_pairs={{0,3},{1,2},{2,1},{3,0},{4,7},{5,6},{6,5},{7,4},{8,11},{9,10},{10,... | collective-permute-start | bytes 589832 | tf_op jit(solution)/shard_map/ppermute | solution.py:88
